TPU v7x, 32 devices: a whole 2x2x4 slice. The times are simulated.
32 devices in a mesh: groups: 2 (over y), atoms: 4 (over z), kvec: 2 (over x), rep: 2 (over core).
Axes of the slice: x: 2, y: 2, z: 4, core: 2. Of those that a mesh axis runs over, the one named last changes fastest.
Arguments:
- positions: float32 [4, 3, 8192], P(('groups', 'rep'), None, 'atoms'), parts along dimension 0, may hold values from 0 to 1
- features: bfloat16 [4, 8192, 256], P(('groups', 'rep'), 'atoms'), parts along dimension 0
- species: int32 [4, 8192], P(('groups', 'rep'), 'atoms'), parts along dimension 0, may hold values from 0 to 7
- cell_length: float32 [4], P(('groups', 'rep')), parts along dimension 0, may hold values from 40 to 60
- energy_ref: float32 [4], P(('groups', 'rep')), parts along dimension 0, may hold values from -12 to -6
- miller_index: int32 [3, 2048], P(None, 'kvec'), may hold values from -8 to 8, as said below
- weight_in: bfloat16 [256, 512], replicated, may hold values from -0.375 to 0.375
- weight_mid: bfloat16 [512, 512], replicated, may hold values from -0.25 to 0.25
- weight_out: bfloat16 [512, 32], replicated, may hold values from -0.25 to 0.25
- species_bias: float32 [8, 512], replicated, may hold values from -3 to 3
Outputs:
- potential: float32 [4, 8192, 32], P(('groups', 'rep'), ('atoms', 'kvec')), parts along dimension 0
- energy: float32 [4], P(('groups', 'rep')), parts along dimension 0
- grad_in: float32 [512, 512], P('groups'), parts along dimension 0
- grad_mid: float32 [1024, 512], P('groups'), parts along dimension 0
- grad_out: float32 [1024, 32], P('groups'), parts along dimension 0
- grad_bias: float32 [16, 512], P('groups'), parts along dimension 0
There are 2 independent parts, one for each index of `groups`. A program takes and returns all parts, laid end to end along the dimension named above; an argument that names none is the same for every part. Nothing has to cross between parts.
Inputs may be any that keep to these rules, and one draw needn't show every extreme that they name: No column of miller_index is all zeros.
All inputs are finite; a program needn't handle non-finite values.
Results may differ from a plain program's by a relative error of at most 0.0046.
Values may be sent and summed in bfloat16 or wider, within the bound.
A program may use at most 64 MiB of HBM per device.

v0:
```python
import math
import jax
import jax.numpy as jnp
from jax import lax
from jax.sharding import PartitionSpec as P

KVECS = 2048
TWO_PI = 2.0 * math.pi
HIGHEST = lax.Precision.HIGHEST


def phase_tiles(coord_rows, miller_float):
    phase_turns = (
        coord_rows[0][:, None] * miller_float[0][None, :]
        + coord_rows[1][:, None] * miller_float[1][None, :]
        + coord_rows[2][:, None] * miller_float[2][None, :]
    )
    phase_angle = TWO_PI * phase_turns
    return jnp.concatenate([jnp.cos(phase_angle), jnp.sin(phase_angle)], axis=1).astype(
        jnp.bfloat16
    )


def wave_weights(miller_float, cell_size, atoms_total):
    index_square = (
        miller_float[0] * miller_float[0]
        + miller_float[1] * miller_float[1]
        + miller_float[2] * miller_float[2]
    )
    factor = TWO_PI / cell_size
    wave_square = index_square * (factor * factor)
    decay_base = jnp.exp(-0.5 * wave_square) / wave_square * (1.0 / math.sqrt(atoms_total * KVECS))
    return jnp.concatenate([decay_base, decay_base])


def contract_rows(left_rows, right_rows):
    return lax.dot_general(
        left_rows, right_rows, (((0,), (0,)), ((), ())), preferred_element_type=jnp.float32
    )


def silu_slope(linear):
    sigmoid_value = jax.nn.sigmoid(linear)
    return sigmoid_value * (1.0 + linear * (1.0 - sigmoid_value))


def forward(atom_features, atom_species, weight_in, weight_mid, weight_out, species_bias):
    kinds = jnp.arange(species_bias.shape[0], dtype=jnp.int32)
    onehot = (atom_species[:, None] == kinds[None, :]).astype(jnp.float32)
    bias_rows = jnp.dot(onehot, species_bias, precision=HIGHEST, preferred_element_type=jnp.float32)
    linear_one = jnp.dot(atom_features, weight_in, preferred_element_type=jnp.float32) + bias_rows
    hidden_one = jax.nn.silu(linear_one).astype(jnp.bfloat16)
    linear_two = jnp.dot(hidden_one, weight_mid, preferred_element_type=jnp.float32)
    hidden_two = jax.nn.silu(linear_two).astype(jnp.bfloat16)
    charges = jnp.dot(hidden_two, weight_out, preferred_element_type=jnp.float32).astype(
        jnp.bfloat16
    )
    return (onehot, linear_one, hidden_one, linear_two, hidden_two, charges)


def backward(
    atom_features,
    onehot,
    linear_one,
    hidden_one,
    linear_two,
    hidden_two,
    grad_charges,
    weight_mid,
    weight_out,
):
    grad_out = contract_rows(hidden_two, grad_charges)
    back_two = lax.dot_general(
        grad_charges, weight_out, (((1,), (1,)), ((), ())), preferred_element_type=jnp.float32
    )
    grad_two = (back_two * silu_slope(linear_two)).astype(jnp.bfloat16)
    grad_mid = contract_rows(hidden_one, grad_two)
    back_one = lax.dot_general(
        grad_two, weight_mid, (((1,), (1,)), ((), ())), preferred_element_type=jnp.float32
    )
    grad_one = (back_one * silu_slope(linear_one)).astype(jnp.bfloat16)
    grad_in = contract_rows(atom_features, grad_one)
    grad_bias = contract_rows(onehot.astype(jnp.bfloat16), grad_one)
    return (grad_in, grad_mid, grad_out, grad_bias)


def body(
    positions,
    features,
    species,
    cell_length,
    energy_ref,
    miller_index,
    weight_in,
    weight_mid,
    weight_out,
    species_bias,
):
    block_rows = positions.shape[2]
    kvec_count = miller_index.shape[1]
    channels = weight_out.shape[1]
    atoms_total = block_rows * lax.axis_size("atoms")
    quarter = block_rows // lax.axis_size("kvec")
    own_first = lax.axis_index("kvec") * quarter
    miller_float = miller_index.astype(jnp.float32)
    column_weights = wave_weights(miller_float, cell_length[0], atoms_total)
    coords = positions[0]
    step_rows = math.gcd(block_rows, 512)
    stored = jnp.concatenate(
        [
            phase_tiles(lax.slice_in_dim(coords, offset, offset + step_rows, axis=1), miller_float)
            for offset in range(0, block_rows, step_rows)
        ],
        axis=0,
    )

    def tile_rows(first_row, row_count):
        return lax.dynamic_slice_in_dim(stored, first_row, row_count, 0)

    zero_panels = jnp.zeros((channels, 2 * kvec_count), jnp.float32)
    own_features = features[0]
    own_species = species[0]
    onehot, linear_one, hidden_one, linear_two, hidden_two, charges = forward(
        own_features, own_species, weight_in, weight_mid, weight_out, species_bias
    )
    running = zero_panels
    row_count = charges.shape[0]
    piece_rows = math.gcd(row_count, 512)
    for inner_start in range(0, row_count, piece_rows):
        phase_rows = tile_rows(0 + inner_start, piece_rows)
        running = running + contract_rows(
            lax.slice_in_dim(charges, inner_start, inner_start + piece_rows, axis=0), phase_rows
        )
    summed = lax.psum(running, "atoms")
    energy_sum = lax.psum(jnp.sum(summed * summed * column_weights[None, :]).reshape(1), "kvec")
    weighted = (summed * column_weights[None, :]).astype(jnp.bfloat16)
    energy = energy_sum / atoms_total
    piece_rows = math.gcd(block_rows, 512)
    pieces = []
    for inner_start in range(0, block_rows, piece_rows):
        phase_rows = tile_rows(0 + inner_start, piece_rows)
        pieces.append(
            lax.dot_general(
                phase_rows, weighted, (((1,), (1,)), ((), ())), preferred_element_type=jnp.float32
            )
        )
    used_potential = lax.psum(jnp.concatenate(pieces, axis=0), "kvec")
    own_potential = lax.dynamic_slice_in_dim(used_potential, own_first, quarter, 0)
    loss_scale = (energy[0] - energy_ref[0]) * (2.0 / atoms_total)
    grad_charges = (loss_scale * used_potential).astype(jnp.bfloat16)
    local_in, local_mid, local_out, local_bias = backward(
        own_features,
        onehot,
        linear_one,
        hidden_one,
        linear_two,
        hidden_two,
        grad_charges,
        weight_mid,
        weight_out,
    )
    grad_in, grad_mid, grad_out, grad_bias = lax.psum(
        (local_in, local_mid, local_out, local_bias), ("atoms", "rep")
    )
    return (own_potential[None], energy, grad_in, grad_mid, grad_out, grad_bias)


def solution(mesh):
    placed = (
        P(("groups", "rep"), None, "atoms"),
        P(("groups", "rep"), "atoms", None),
        P(("groups", "rep"), "atoms"),
        P(("groups", "rep")),
        P(("groups", "rep")),
        P(None, "kvec"),
        P(),
        P(),
        P(),
        P(),
    )
    return jax.shard_map(
        body,
        mesh=mesh,
        in_specs=placed,
        out_specs=(
            P(("groups", "rep"), ("atoms", "kvec"), None),
            P(("groups", "rep")),
            P("groups", None),
            P("groups", None),
            P("groups", None),
            P("groups", None),
        ),
        check_vma=False,
    )
```

profile of v0, /device:TPU:0, one launch (start us, length us, event | category | flops | bytes accessed | tf_op | source)
XLA Modules:
  0.0 213.0 jit_solution(59138224484041995)
XLA Ops:
  7.2 0.0 copy-start
  7.2 0.0 all-reduce.5.cloned.1.call-start
  7.2 0.8 convert_element_type.34
  8.0 0.8 copy.19
  8.8 0.0 copy-done
  8.8 0.0 copy-start.16
  8.8 0.0 copy-start.19
  8.9 1.7 fusion.6
  10.5 0.0 copy-done.16
  10.5 0.0 copy-done.19
  10.6 0.0 copy-start.17
  10.6 4.2 %multiply_convert_fusion.3 = (bf16[2048,512]{1,0:T(8,128)(2,1)S(1)}, f32[2048,512]{1,0:T(8,128)}) fusion(f32[2048,512]{1,0:T(8,128)S(1)} %fusion.6, f32[8,512]{1,0:T(8,128)S(1)} %copy-done.19, s32[2048]{0:T(1024)S(1)} %bitcast.56), kind=kOutput, calls=%fused_computation.4 | convolution fusion | flops 106971136 | bytes 10510336 | tf_op jit(solution)/shard_map/dot_general | solution.py:50
  14.8 3.8 %multiply_convert_fusion.2 = (bf16[2048,512]{1,0:T(8,128)(2,1)S(1)}, f32[2048,512]{1,0:T(8,128)}) fusion(bf16[2048,512]{1,0:T(8,128)(2,1)S(1)} %get-tuple-element.46, bf16[512,512]{1,0:T(8,128)(2,1)S(1)} %copy-done.17), kind=kOutput, calls=%fused_computation.2 | convolution fusion | flops 1078984704 | bytes 8912896 | tf_op jit(solution)/shard_map/dot_general | solution.py:53
  18.5 0.7 convolution_convert_fusion
  19.2 33.6 %cosine_convert_fusion = (bf16[512,1024]{1,0:T(8,128)(2,1)S(1)}, bf16[512,1024]{1,0:T(8,128)(2,1)S(1)}, bf16[512,1024]{1,0:T(8,128)(2,1)S(1)}, bf16[512,1024]{1,...) fusion(f32[512]{0:T(512)S(1)} %bitcast.59, ...), kind=kLoop, calls=%fused_computation.16 | loop fusion | flops 16777216 | bytes 8425472 | tf_op jit(solution)/shard_map/convert
  52.8 0.0 copy-done.1
  52.8 0.0 copy-start.3
  52.8 0.0 copy-start.5
  52.8 0.0 copy-start.7
  52.9 0.0 copy-start.9
  52.9 0.0 copy-start.11
  52.9 0.0 copy-start.12
  52.9 0.5 fusion.4
  53.4 0.5 convolution_add_fusion.3
  53.8 0.0 copy-done.3
  53.9 0.3 copy-done.5
  54.2 0.3 copy-done.7
  54.5 0.3 copy-done.9
  54.8 0.5 convolution_add_fusion.2
  55.2 0.0 copy-done.11
  55.2 0.2 copy-done.12
  55.5 1.2 convolution_add_fusion.1
  56.7 0.0 all-reduce.5.cloned.1.call-update
  56.7 0.0 all-reduce.7.cloned.1.call-start
  57.5 37.4 %all-reduce.5.cloned.1.call-done = f32[32,2048]{1,0:T(8,128)} async-done(((f32[32,2048]{1,0:T(8,128)}), f32[32,2048]{1,0:T(8,128)}) %all-reduce.5.cloned.1.call-update) | async-done | bytes 262160 | tf_op jit(solution)/shard_map/psum | solution.py:134
  94.8 1.8 multiply_reduce_fusion
  96.6 2.3 %fusion = f32[512,32]{0,1:T(8,128)S(1)} fusion(bf16[32,2048]{1,0:T(8,128)(2,1)S(1)} %get-tuple-element.16, bf16[512,1024]{1,0:T(8,128)(2,1)} %copy-done.12, bf16[512,1024]{1,0:T(8,128)(2,1)} %copy-done.11), kind=kOutput, calls=%fused_computation.27 | convolution fusion | flops 71303168 | bytes 2293760 | tf_op jit(solution)/shard_map/dot_general | solution.py:143
  98.9 0.0 copy-done.8
  98.9 0.7 fusion.1
  99.6 0.5 copy-done.4
  100.1 0.3 copy-done.6
  100.4 0.7 fusion.2
  101.2 0.7 fusion.3
  101.9 0.7 pad_maximum_fusion.12
  102.7 0.0 all-reduce.7.cloned.1.call-update
  102.7 0.0 all-reduce.9.cloned.1.call-start
  103.4 5.6 %psum.51 = f32[1]{0:T(128)} all-reduce(f32[1]{0:T(128)} %bitcast.19), channel_id=1, replica_groups=mesh['groups'=2,'atoms'=4,'kvec'=2,'rep'=2] {'kvec'}, use_global_device_ids=true, to_apply=%region_3.4 | all-reduce | flops 1 | bytes 8 | tf_op jit(solution)/shard_map/psum | solution.py:135
  109.6 16.1 %all-reduce.7.cloned.1.call-done = f32[2048,32]{0,1:T(8,128)} async-done(((f32[2048,32]{0,1:T(8,128)}), f32[2048,32]{0,1:T(8,128)}) %all-reduce.7.cloned.1.call-update) | async-done | bytes 262160 | tf_op jit(solution)/shard_map/psum | solution.py:147
  125.8 4.2 %multiply_convert_fusion.1 = bf16[2048,512]{1,0:T(8,128)(2,1)S(1)} fusion(f32[2048,512]{1,0:T(8,128)} %get-tuple-element.49, bf16[512,32]{0,1:T(8,128)(2,1)S(1)} %copy-done.15, f32[2048,32]{0,1:T(8,128)} %all-reduce.7.cloned.1.call-done, f32[]{:T(128)} %bitcast.20), kind=kOutput, calls=%fused_computation.1 | convolution fusion | flops 76677120 | bytes 6586372 | tf_op jit(solution)/shard_map/dot_general | solution.py:73
  129.9 0.0 copy-start.18
  130.0 2.3 %fusion.26 = f32[512,512]{1,0:T(8,128)} fusion(bf16[2048,512]{1,0:T(8,128)(2,1)S(1)} %copy-done.21, bf16[2048,512]{1,0:T(8,128)(2,1)S(1)} %multiply_convert_fusion.1), kind=kOutput, calls=%fused_computation.64 | convolution fusion | flops 1073741824 | bytes 5242880 | tf_op jit(solution)/shard_map/dot_general | solution.py:37
  132.2 0.3 copy-done.22
  132.5 2.3 %multiply_convert_fusion = bf16[2048,512]{1,0:T(8,128)(2,1)S(1)} fusion(f32[2048,512]{1,0:T(8,128)S(1)} %copy-done.22, bf16[2048,512]{1,0:T(8,128)(2,1)S(1)} %multiply_convert_fusion.1, bf16[512,512]{1,0:T(8,128)(2,1)S(1)} %copy-done.18), kind=kOutput, calls=%fused_computation | convolution fusion | flops 1083179008 | bytes 8912896 | tf_op jit(solution)/shard_map/dot_general | solution.py:78
  134.9 1.5 convolution_bitcast_fusion
  136.5 0.0 copy-done.2
  136.5 1.1 fusion.11
  137.6 0.0 all-reduce.9.cloned.1.call-update
  137.6 0.8 fusion.8
  138.4 29.5 %psum.55 = f32[8,512]{1,0:T(8,128)} all-reduce(f32[8,512]{1,0:T(8,128)S(1)} %fusion.8), channel_id=1, replica_groups=mesh['groups'=2,'atoms'=4,'kvec'=2,'rep'=2] {'atoms','rep'}, use_global_device_ids=true, to_apply=%region_7.8 | all-reduce | flops 4096 | bytes 32768 | tf_op jit(solution)/shard_map/psum | solution.py:162
  167.9 0.7 dynamic-slice_bitcast_fusion
  168.6 31.8 %all-reduce.9.cloned.1.call-done = (f32[256,512]{0,1:T(8,128)}, f32[512,512]{1,0:T(8,128)}, f32[512,32]{0,1:T(8,128)}) async-done(((f32[256,512]{0,1:T(8,128)}, f32[512,512]{1,0:T(8,128)}, f32[512,32]{0,1:T(8,128)}), (f32[256,512]{0,1:T(8,128)}, f32[512,512]{1,0:T(8,128)}, f32[512,32]{0,1:T(8,128)})) %all-reduce.9.cloned.1.call-update) | async-done | bytes 1638416 | tf_op jit(solution)/shard_map/psum | solution.py:162
  200.3 2.1 copy.16
  202.4 2.3 %copy.27 = f32[512,512]{1,0:T(8,128)} copy(f32[512,512]{1,0:T(8,128)} %get-tuple-element.53) | data formatting | bytes 2097152
  204.7 0.6 copy.28
  (24 shorter events, 0.1 us)
Async XLA Ops:
  7.2 1.7 copy-start
  7.2 87.7 %all-reduce.5.cloned.1.call-start = ((), (), s32[]{:S(2)}) async-start(), calls=%async_computation | async-start | bytes 524288 | tf_op jit(solution)/shard_map/psum | solution.py:134
  8.8 1.7 copy-start.16
  8.8 1.7 copy-start.19
  10.6 4.2 %copy-start.17 = (bf16[512,512]{1,0:T(8,128)(2,1)S(1)}, bf16[512,512]{1,0:T(8,128)(2,1)}, u32[]{:S(2)}) copy-start(bf16[512,512]{1,0:T(8,128)(2,1)} %param.17) | copy-start | bytes 1572868
  14.8 3.8 %copy-start.20 = (bf16[2048,512]{1,0:T(8,128)(2,1)}, bf16[2048,512]{1,0:T(8,128)(2,1)S(1)}, u32[]{:S(2)}) copy-start(bf16[2048,512]{1,0:T(8,128)(2,1)S(1)} %get-tuple-element.46) | copy-start | bytes 6291460
  14.8 3.8 %copy-start.15 = (bf16[512,32]{0,1:T(8,128)(2,1)S(1)}, bf16[512,32]{0,1:T(8,128)(2,1)}, u32[]{:S(2)}) copy-start(bf16[512,32]{0,1:T(8,128)(2,1)} %param.18) | copy-start | bytes 98308
  18.5 34.3 %copy-start.1 = (bf16[2048,512]{1,0:T(8,128)(2,1)}, bf16[2048,512]{1,0:T(8,128)(2,1)S(1)}, u32[]{:S(2)}) copy-start(bf16[2048,512]{1,0:T(8,128)(2,1)S(1)} %get-tuple-element.48) | copy-start | bytes 6291460
  52.8 1.0 copy-start.3
  52.8 1.3 copy-start.5
  52.8 1.6 copy-start.7
  52.9 1.9 copy-start.9
  52.9 2.4 %copy-start.11 = (bf16[512,1024]{1,0:T(8,128)(2,1)}, bf16[512,1024]{1,0:T(8,128)(2,1)S(1)}, u32[]{:S(2)}) copy-start(bf16[512,1024]{1,0:T(8,128)(2,1)S(1)} %get-tuple-element.29) | copy-start | bytes 3145732
  52.9 2.6 %copy-start.12 = (bf16[512,1024]{1,0:T(8,128)(2,1)}, bf16[512,1024]{1,0:T(8,128)(2,1)S(1)}, u32[]{:S(2)}) copy-start(bf16[512,1024]{1,0:T(8,128)(2,1)S(1)} %get-tuple-element.30) | copy-start | bytes 3145732
  56.7 69.1 %all-reduce.7.cloned.1.call-start = ((), (), s32[]{:S(2)}) async-start(), calls=%async_computation.1 | async-start | bytes 524288 | tf_op jit(solution)/shard_map/psum | solution.py:147
  94.8 4.1 %copy-start.8 = (bf16[512,1024]{1,0:T(8,128)(2,1)S(1)}, bf16[512,1024]{1,0:T(8,128)(2,1)}, u32[]{:S(2)}) copy-start(bf16[512,1024]{1,0:T(8,128)(2,1)} %copy-done.7) | copy-start | bytes 3145732
  94.8 4.1 %copy-start.10 = (bf16[512,1024]{1,0:T(8,128)(2,1)S(1)}, bf16[512,1024]{1,0:T(8,128)(2,1)}, u32[]{:S(2)}) copy-start(bf16[512,1024]{1,0:T(8,128)(2,1)} %copy-done.9) | copy-start | bytes 3145732
  98.9 1.2 copy-start.4
  98.9 1.5 copy-start.6
  102.7 97.7 %all-reduce.9.cloned.1.call-start = ((), (), s32[]{:S(2)}) async-start(), calls=%async_computation.2 | async-start | bytes 3276800 | tf_op jit(solution)/shard_map/psum | solution.py:162
  125.8 4.2 %copy-start.21 = (bf16[2048,512]{1,0:T(8,128)(2,1)S(1)}, bf16[2048,512]{1,0:T(8,128)(2,1)}, u32[]{:S(2)}) copy-start(bf16[2048,512]{1,0:T(8,128)(2,1)} %copy-done.20) | copy-start | bytes 6291460
  129.9 2.3 %copy-start.18 = (bf16[512,512]{1,0:T(8,128)(2,1)S(1)}, bf16[512,512]{1,0:T(8,128)(2,1)}, u32[]{:S(2)}) copy-start(bf16[512,512]{1,0:T(8,128)(2,1)} %param.17) | copy-start | bytes 1572868
  130.0 2.6 %copy-start.22 = (f32[2048,512]{1,0:T(8,128)S(1)}, f32[2048,512]{1,0:T(8,128)}, u32[]{:S(2)}) copy-start(f32[2048,512]{1,0:T(8,128)} %get-tuple-element.47) | copy-start | bytes 12582916
  134.9 1.6 copy-start.2
  134.9 1.6 copy-start.13
  200.3 4.3 %copy-start.14 = (f32[512,32]{0,1:T(8,128)S(1)}, f32[512,32]{0,1:T(8,128)}, u32[]{:S(2)}) copy-start(f32[512,32]{0,1:T(8,128)} %get-tuple-element.54) | copy-start | bytes 196612
Sparse Core Ops, SparseCore 0:
  56.8 37.9 all-reduce.4
  102.8 22.9 all-reduce.6
  137.7 62.5 all-reduce.8
where the time goes:
time: 213 us
  waiting for transfers between devices  85.4 us (40%)
  other arithmetic  36.9 us (17%)
  blocking collectives  35.1 us (16%)
  matrix products  29.5 us (14%)
  between operations  17.1 us (8%)
  local copies, waits for them, and re-layouts  8.84 us (4%)
    psum x1, waiting for transfers between devices, body(): summed = lax.psum(running, 'atoms')  37.4 us
    another operation x1, other arithmetic  33.6 us
    psum x1, waiting for transfers between devices, body(): lax.psum((local_in, local_mid, local_out, local_bias), ('atoms', 'rep'))  31.8 us
    psum x1, blocking collectives, body(): lax.psum((local_in, local_mid, local_out, local_bias), ('atoms', 'rep'))  29.5 us
    psum x1, waiting for transfers between devices, body(): used_potential = lax.psum(jnp.concatenate(pieces, axis=0), 'kvec')  16.1 us
    dot_general x8, matrix products, contract_rows(): lax.dot_general(left_rows, right_rows, (((0,), (0,)), ((), ())), preferre...  8.23 us
    unnamed x50, local copies, waits for them, and re-layouts  8.15 us
    psum x1, blocking collectives, body(): lax.psum(jnp.sum(summed * summed * column_weights[None, :]).reshape(1), '...  5.58 us
  transfers between devices with their start and end apart: 3, of which 3 were waited for; matrix products, arithmetic and copies ran while one was open for 1% of the time, Pallas kernels for 0%

commit v1 on v0

--- a/solution.py
+++ b/solution.py
@@ -7,6 +7,11 @@
 KVECS = 2048
 TWO_PI = 2.0 * math.pi
 HIGHEST = lax.Precision.HIGHEST
+
+
+def one_after_other(value, axis_one, axis_two):
+    inner = lax.psum(value, axis_one)
+    return lax.psum(inner, axis_two)
 
 
 def phase_tiles(coord_rows, miller_float):
@@ -159,8 +164,8 @@
         weight_mid,
         weight_out,
     )
-    grad_in, grad_mid, grad_out, grad_bias = lax.psum(
-        (local_in, local_mid, local_out, local_bias), ("atoms", "rep")
+    grad_in, grad_mid, grad_out, grad_bias = one_after_other(
+        (local_in, local_mid, local_out, local_bias), "rep", "atoms"
     )
     return (own_potential[None], energy, grad_in, grad_mid, grad_out, grad_bias)
 

time: 213 us -> 248 us (1.16)
  waiting for transfers between devices: 85.4 us -> 125 us
  blocking collectives: 35.1 us -> 29.3 us
    psum x1 -> x2, waiting for transfers between devices: 31.8 us -> 71.8 us  [the longest x1 51 us: one_after_other(): return lax.psum(inner, axis_two)]
    psum x1 -> x2, blocking collectives: 29.5 us -> 23.8 us  [the longest x1 20.4 us: one_after_other(): return lax.psum(inner, axis_two)]
  transfers between devices with their start and end apart: 3 -> 4, of which waited for: 3 -> 4; matrix products, arithmetic and copies ran while one was open for 1% -> 1% of each run, Pallas kernels for 0% -> 0%
where the time goes in v1:
time: 248 us; the launch traced here: 247 us
  waiting for transfers between devices  125 us (50%)
  other arithmetic  36.9 us (15%)
  matrix products  29.6 us (12%)
  blocking collectives  29.3 us (12%)
  between operations  17.2 us (7%)
  local copies, waits for them, and re-layouts  8.84 us (4%)
    psum x1, waiting for transfers between devices, one_after_other(): return lax.psum(inner, axis_two)  51 us
    psum x1, waiting for transfers between devices, body(): summed = lax.psum(running, 'atoms')  37.4 us
    another operation x1, other arithmetic  33.6 us
    psum x1, waiting for transfers between devices, one_after_other(): inner = lax.psum(value, axis_one)  20.8 us
    psum x1, blocking collectives, one_after_other(): return lax.psum(inner, axis_two)  20.4 us
    psum x1, waiting for transfers between devices, body(): used_potential = lax.psum(jnp.concatenate(pieces, axis=0), 'kvec')  16.1 us
    dot_general x8, matrix products, contract_rows(): lax.dot_general(left_rows, right_rows, (((0,), (0,)), ((), ())), preferre...  8.23 us
    unnamed x50, local copies, waits for them, and re-layouts  8.14 us
  transfers between devices with their start and end apart: 4, of which 4 were waited for; matrix products, arithmetic and copies ran while one was open for 1% of the time, Pallas kernels for 0%

profile of v1, /device:TPU:0, one launch (start us, length us, event | category | flops | bytes accessed | tf_op | source)
XLA Modules:
  0.0 247.3 jit_solution(17283530213473628190)
XLA Ops:
  7.2 0.0 copy-start
  7.2 0.0 all-reduce.7.cloned.1.call-start
  7.2 0.8 convert_element_type.34
  8.0 0.8 copy.19
  8.8 0.0 copy-done
  8.8 0.0 copy-start.16
  8.8 0.0 copy-start.19
  8.9 1.7 fusion.6
  10.5 0.0 copy-done.16
  10.5 0.0 copy-done.19
  10.6 0.0 copy-start.17
  10.6 4.2 %multiply_convert_fusion.3 = (bf16[2048,512]{1,0:T(8,128)(2,1)S(1)}, f32[2048,512]{1,0:T(8,128)}) fusion(f32[2048,512]{1,0:T(8,128)S(1)} %fusion.6, f32[8,512]{1,0:T(8,128)S(1)} %copy-done.19, s32[2048]{0:T(1024)S(1)} %bitcast.56), kind=kOutput, calls=%fused_computation.4 | convolution fusion | flops 106971136 | bytes 10510336 | tf_op jit(solution)/shard_map/dot_general | solution.py:55
  14.8 0.0 copy-done.17
  14.8 3.8 %multiply_convert_fusion.2 = (bf16[2048,512]{1,0:T(8,128)(2,1)S(1)}, f32[2048,512]{1,0:T(8,128)}) fusion(bf16[2048,512]{1,0:T(8,128)(2,1)S(1)} %get-tuple-element.49, bf16[512,512]{1,0:T(8,128)(2,1)S(1)} %copy-done.17), kind=kOutput, calls=%fused_computation.2 | convolution fusion | flops 1078984704 | bytes 8912896 | tf_op jit(solution)/shard_map/dot_general | solution.py:58
  18.6 0.7 convolution_convert_fusion
  19.3 33.6 %cosine_convert_fusion = (bf16[512,1024]{1,0:T(8,128)(2,1)S(1)}, bf16[512,1024]{1,0:T(8,128)(2,1)S(1)}, bf16[512,1024]{1,0:T(8,128)(2,1)S(1)}, bf16[512,1024]{1,...) fusion(f32[512]{0:T(512)S(1)} %bitcast.59, ...), kind=kLoop, calls=%fused_computation.16 | loop fusion | flops 16777216 | bytes 8425472 | tf_op jit(solution)/shard_map/convert
  52.8 0.0 copy-done.1
  52.9 0.0 copy-start.12
  52.9 0.5 fusion.4
  53.4 0.5 convolution_add_fusion.3
  53.8 0.0 copy-done.3
  53.9 0.3 copy-done.5
  54.2 0.3 copy-done.7
  54.5 0.3 copy-done.9
  54.8 0.5 convolution_add_fusion.2
  55.3 0.0 copy-done.11
  55.3 0.2 copy-done.12
  55.5 1.2 convolution_add_fusion.1
  56.7 0.0 all-reduce.7.cloned.1.call-update
  56.7 0.0 all-reduce.9.cloned.1.call-start
  57.5 37.4 %all-reduce.7.cloned.1.call-done = f32[32,2048]{1,0:T(8,128)} async-done(((f32[32,2048]{1,0:T(8,128)}), f32[32,2048]{1,0:T(8,128)}) %all-reduce.7.cloned.1.call-update) | async-done | bytes 262160 | tf_op jit(solution)/shard_map/psum | solution.py:139
  94.8 1.8 multiply_reduce_fusion
  96.6 2.3 fusion
  98.9 0.0 copy-done.8
  98.9 0.7 fusion.1
  99.7 0.5 copy-done.4
  100.1 0.3 copy-done.6
  100.5 0.7 fusion.2
  101.2 0.7 fusion.3
  101.9 0.7 pad_maximum_fusion.12
  102.7 0.0 all-reduce.9.cloned.1.call-update
  102.7 0.0 all-reduce.13.cloned.1.call-start
  103.4 5.6 %psum.79 = f32[1]{0:T(128)} all-reduce(f32[1]{0:T(128)} %bitcast.19), channel_id=1, replica_groups=mesh['groups'=2,'atoms'=4,'kvec'=2,'rep'=2] {'kvec'}, use_global_device_ids=true, to_apply=%region_3.4 | all-reduce | flops 1 | bytes 8 | tf_op jit(solution)/shard_map/psum | solution.py:140
  109.6 16.1 %all-reduce.9.cloned.1.call-done = f32[2048,32]{0,1:T(8,128)} async-done(((f32[2048,32]{0,1:T(8,128)}), f32[2048,32]{0,1:T(8,128)}) %all-reduce.9.cloned.1.call-update) | async-done | bytes 262160 | tf_op jit(solution)/shard_map/psum | solution.py:152
  125.8 4.2 %multiply_convert_fusion.1 = bf16[2048,512]{1,0:T(8,128)(2,1)S(1)} fusion(f32[2048,512]{1,0:T(8,128)} %get-tuple-element.52, bf16[512,32]{0,1:T(8,128)(2,1)S(1)} %copy-done.15, f32[2048,32]{0,1:T(8,128)} %all-reduce.9.cloned.1.call-done, f32[]{:T(128)} %bitcast.20), kind=kOutput, calls=%fused_computation.1 | convolution fusion | flops 76677120 | bytes 6586372 | tf_op jit(solution)/shard_map/dot_general | solution.py:78
  130.0 0.0 copy-start.18
  130.0 2.3 fusion.26
  132.3 0.3 copy-done.22
  132.6 2.3 multiply_convert_fusion
  135.0 1.5 convolution_bitcast_fusion
  136.5 0.0 copy-done.2
  136.5 1.1 fusion.11
  137.6 0.0 all-reduce.13.cloned.1.call-update
  137.7 0.0 all-reduce.11.cloned.1.call-start
  137.7 20.8 %all-reduce.13.cloned.1.call-done = (f32[256,512]{0,1:T(8,128)}, f32[512,512]{1,0:T(8,128)}, f32[512,32]{0,1:T(8,128)}) async-done(((f32[256,512]{0,1:T(8,128)}, f32[512,512]{1,0:T(8,128)}, f32[512,32]{0,1:T(8,128)}), (f32[256,512]{0,1:T(8,128)}, f32[512,512]{1,0:T(8,128)}, f32[512,32]{0,1:T(8,128)})) %all-reduce.13.cloned.1.call-update) | async-done | bytes 1638416 | tf_op jit(solution)/shard_map/psum | solution.py:13
  158.5 0.0 all-reduce.11.cloned.1.call-update
  158.5 0.8 fusion.8
  159.3 3.4 %psum.86 = f32[8,512]{1,0:T(8,128)S(1)} all-reduce(f32[8,512]{1,0:T(8,128)S(1)} %fusion.8), channel_id=1, replica_groups=mesh['groups'=2,'atoms'=4,'kvec'=2,'rep'=2] {'rep'}, use_global_device_ids=true, to_apply=%region_10.11 | all-reduce | flops 4096 | bytes 32768 | tf_op jit(solution)/shard_map/psum | solution.py:13
  162.7 20.4 %psum.87 = f32[8,512]{1,0:T(8,128)} all-reduce(f32[8,512]{1,0:T(8,128)S(1)} %psum.86), channel_id=1, replica_groups=mesh['groups'=2,'atoms'=4,'kvec'=2,'rep'=2] {'atoms'}, use_global_device_ids=true, to_apply=%region_11.12 | all-reduce | flops 4096 | bytes 32768 | tf_op jit(solution)/shard_map/psum | solution.py:14
  183.0 0.7 dynamic-slice_bitcast_fusion
  183.7 51.0 %all-reduce.11.cloned.1.call-done = (f32[256,512]{0,1:T(8,128)}, f32[512,512]{1,0:T(8,128)}, f32[512,32]{0,1:T(8,128)}) async-done(((f32[256,512]{0,1:T(8,128)}, f32[512,512]{1,0:T(8,128)}, f32[512,32]{0,1:T(8,128)}), (f32[256,512]{0,1:T(8,128)}, f32[512,512]{1,0:T(8,128)}, f32[512,32]{0,1:T(8,128)})) %all-reduce.11.cloned.1.call-update) | async-done | bytes 1638416 | tf_op jit(solution)/shard_map/psum | solution.py:14
  234.7 2.1 copy.16
  236.8 2.3 copy.30
  239.0 0.6 copy.31
  (28 shorter events, 0.1 us)
Async XLA Ops:
  7.2 1.7 copy-start
  7.2 87.7 %all-reduce.7.cloned.1.call-start = ((), (), s32[]{:S(2)}) async-start(), calls=%async_computation | async-start | bytes 524288 | tf_op jit(solution)/shard_map/psum | solution.py:139
  8.8 1.7 copy-start.16
  8.8 1.7 copy-start.19
  10.6 4.2 %copy-start.17 = (bf16[512,512]{1,0:T(8,128)(2,1)S(1)}, bf16[512,512]{1,0:T(8,128)(2,1)}, u32[]{:S(2)}) copy-start(bf16[512,512]{1,0:T(8,128)(2,1)} %param.17) | copy-start | bytes 1572868
  14.8 3.8 %copy-start.20 = (bf16[2048,512]{1,0:T(8,128)(2,1)}, bf16[2048,512]{1,0:T(8,128)(2,1)S(1)}, u32[]{:S(2)}) copy-start(bf16[2048,512]{1,0:T(8,128)(2,1)S(1)} %get-tuple-element.49) | copy-start | bytes 6291460
  14.8 3.8 %copy-start.15 = (bf16[512,32]{0,1:T(8,128)(2,1)S(1)}, bf16[512,32]{0,1:T(8,128)(2,1)}, u32[]{:S(2)}) copy-start(bf16[512,32]{0,1:T(8,128)(2,1)} %param.18) | copy-start | bytes 98308
  18.5 34.3 %copy-start.1 = (bf16[2048,512]{1,0:T(8,128)(2,1)}, bf16[2048,512]{1,0:T(8,128)(2,1)S(1)}, u32[]{:S(2)}) copy-start(bf16[2048,512]{1,0:T(8,128)(2,1)S(1)} %get-tuple-element.51) | copy-start | bytes 6291460
  52.8 1.0 copy-start.3
  52.9 1.3 copy-start.5
  52.9 1.6 copy-start.7
  52.9 1.9 copy-start.9
  52.9 2.4 copy-start.11
  52.9 2.6 %copy-start.12 = (bf16[512,1024]{1,0:T(8,128)(2,1)}, bf16[512,1024]{1,0:T(8,128)(2,1)S(1)}, u32[]{:S(2)}) copy-start(bf16[512,1024]{1,0:T(8,128)(2,1)S(1)} %get-tuple-element.33) | copy-start | bytes 3145732
  56.7 69.1 %all-reduce.9.cloned.1.call-start = ((), (), s32[]{:S(2)}) async-start(), calls=%async_computation.1 | async-start | bytes 524288 | tf_op jit(solution)/shard_map/psum | solution.py:152
  94.8 4.1 %copy-start.8 = (bf16[512,1024]{1,0:T(8,128)(2,1)S(1)}, bf16[512,1024]{1,0:T(8,128)(2,1)}, u32[]{:S(2)}) copy-start(bf16[512,1024]{1,0:T(8,128)(2,1)} %copy-done.7) | copy-start | bytes 3145732
  94.8 4.1 %copy-start.10 = (bf16[512,1024]{1,0:T(8,128)(2,1)S(1)}, bf16[512,1024]{1,0:T(8,128)(2,1)}, u32[]{:S(2)}) copy-start(bf16[512,1024]{1,0:T(8,128)(2,1)} %copy-done.9) | copy-start | bytes 3145732
  98.9 1.2 copy-start.4
  98.9 1.5 copy-start.6
  102.7 55.8 %all-reduce.13.cloned.1.call-start = ((), (), s32[]{:S(2)}) async-start(), calls=%async_computation.3 | async-start | bytes 3276800 | tf_op jit(solution)/shard_map/psum | solution.py:13
  125.8 4.2 %copy-start.21 = (bf16[2048,512]{1,0:T(8,128)(2,1)S(1)}, bf16[2048,512]{1,0:T(8,128)(2,1)}, u32[]{:S(2)}) copy-start(bf16[2048,512]{1,0:T(8,128)(2,1)} %copy-done.20) | copy-start | bytes 6291460
  130.0 2.3 copy-start.18
  130.0 2.6 %copy-start.22 = (f32[2048,512]{1,0:T(8,128)S(1)}, f32[2048,512]{1,0:T(8,128)}, u32[]{:S(2)}) copy-start(f32[2048,512]{1,0:T(8,128)} %get-tuple-element.50) | copy-start | bytes 12582916
  134.9 1.6 copy-start.2
  134.9 1.6 copy-start.13
  137.7 97.0 %all-reduce.11.cloned.1.call-start = ((), (), s32[]{:S(2)}) async-start(), calls=%async_computation.2 | async-start | bytes 3276800 | tf_op jit(solution)/shard_map/psum | solution.py:14
  234.7 4.3 %copy-start.14 = (f32[512,32]{0,1:T(8,128)S(1)}, f32[512,32]{0,1:T(8,128)}, u32[]{:S(2)}) copy-start(f32[512,32]{0,1:T(8,128)} %get-tuple-element.57) | copy-start | bytes 196612
Sparse Core Ops, SparseCore 0:
  56.8 37.9 all-reduce.6
  102.8 22.9 all-reduce.8
  137.8 20.6 all-reduce.12
  161.1 73.5 all-reduce.10
